TPU v7x, 32 devices: a whole 2x2x4 slice. The times are simulated.
32 devices in a mesh: section: 4 (over y, x), dp: 8 (over z, core).
Axes of the slice: x: 2, y: 2, z: 4, core: 2. Of those that a mesh axis runs over, the one named last changes fastest.
Arguments:
- frozen: bfloat16 [4, 8192, 8192], P('section', 'dp'), may hold values from -0.0625 to 0.0625
- adapt_down: bfloat16 [4, 16, 8192, 64], P('section', 'dp'), may hold values from -0.0625 to 0.0625
- adapt_up: bfloat16 [4, 16, 64, 8192], P('section', 'dp'), may hold values from -0.0625 to 0.0625
- saved_inputs: bfloat16 [4, 1, 24, 8192], P('section', None, None, 'dp'), may hold values from -6 to 6
- out_grad: bfloat16 [1, 24, 8192], P(None, None, 'dp'), may hold values from -6 to 6
- sensor: int32 [1, 8], replicated, may hold values from 0 to 15, as said below
- counts: int32 [16], P('dp'), may hold values from 256 to 2047
Outputs:
- in_grad: bfloat16 [4, 1, 24, 8192], P('section', None, None, 'dp')
- grad_down: bfloat16 [4, 16, 8192, 64], P('section', 'dp')
- grad_up: bfloat16 [4, 16, 64, 8192], P('section', 'dp')
Inputs may be any that keep to these rules, and one draw needn't show every extreme that they name: `sensor`: in each micro-batch at most 2 blocks have sensors s with s // 2 equal to one given value, and exactly 2 for some value.
All inputs are finite; a program needn't handle non-finite values.
Results may differ from a plain program's by a relative error of at most 0.013.
Values may be sent and summed in bfloat16 or wider, within the bound.
A program may use at most 128 MiB of HBM per device.

v0:
```python
import math

import jax
import jax.numpy as jnp
from jax import lax
from jax.sharding import PartitionSpec as P

CAP = 2


SCALE = 2.0
NORM_TOK = 1024.0
CLIP_RMS = 0.5


def passed_along(array, axis, by):
    length = lax.axis_size(axis)
    pairs = [(i, i + by) for i in range(length) if 0 <= i + by < length]
    return lax.ppermute(array, axis, pairs)


def placement_rows(owner_row, block_rows, devices):
    same = owner_row[:, None] == owner_row[None, :]
    order = jnp.arange(devices, dtype=jnp.int32)
    earlier = order[:, None] < order[None, :]
    position = jnp.sum((same & earlier).astype(jnp.int32), axis=0)
    first = (owner_row * CAP + position) * block_rows
    target = (first[:, None] + jnp.arange(block_rows, dtype=jnp.int32)[None, :]).reshape(-1)
    slots = jnp.arange(devices * CAP * block_rows, dtype=jnp.int32)
    return (target[:, None] == slots[None, :]).astype(jnp.bfloat16)


def per_device(frozen, adapt_down, adapt_up, saved_inputs, out_grad, sensor, counts):
    n_dp = lax.axis_size("dp")
    n_section = lax.axis_size("section")
    section_index = lax.axis_index("section")
    my_index = lax.axis_index("dp")
    w_rows = frozen[0]
    down_local = adapt_down[0]
    up_local = adapt_up[0]
    inputs_all = saved_inputs[0]
    micro = out_grad.shape[0]
    tokens = out_grad.shape[1]
    columns = out_grad.shape[2]
    width = columns * n_dp
    block_rows = tokens // n_dp
    sen_local = down_local.shape[0]
    rank = down_local.shape[2]
    slot_rows = CAP * block_rows

    def step(turn, carry):
        received, acc_down, acc_up, in_grad = carry
        micro_index = turn - (n_section - 1 - section_index)
        valid = (micro_index >= 0) & (micro_index < micro)
        safe = jnp.clip(micro_index, 0, micro - 1)
        incoming = lax.dynamic_index_in_dim(out_grad, safe, 0, keepdims=False)
        current = jnp.where(section_index == n_section - 1, incoming, received)
        inputs_cols = lax.dynamic_index_in_dim(inputs_all, safe, 0, keepdims=False)
        idents = lax.dynamic_index_in_dim(sensor, safe, 0, keepdims=False)
        owners = idents // sen_local
        place = placement_rows(owners, block_rows, n_dp)
        select = lax.dynamic_slice_in_dim(place, my_index * slot_rows, slot_rows, 1).T
        grad_full, input_full = (
            lax.all_gather(current, "dp", axis=1, tiled=True),
            lax.all_gather(inputs_cols, "dp", axis=1, tiled=True),
        )
        input_sel = jnp.dot(select, input_full, preferred_element_type=jnp.float32).astype(
            jnp.bfloat16
        )
        grad_sel = jnp.dot(select, grad_full, preferred_element_type=jnp.float32).astype(
            jnp.bfloat16
        )
        local_ident = jnp.repeat(idents % sen_local, block_rows)
        which = (local_ident[:, None] == jnp.arange(sen_local, dtype=jnp.int32)[None, :]).astype(
            jnp.bfloat16
        )
        masks = jnp.dot(select, which, preferred_element_type=jnp.float32).T
        up_proj = jnp.einsum("rd,skd->srk", grad_sel, up_local, preferred_element_type=jnp.float32)
        lowu = jnp.sum(masks[:, :, None] * up_proj, axis=0).astype(jnp.bfloat16)
        down_proj = jnp.einsum(
            "rd,sdk->srk", input_sel, down_local, preferred_element_type=jnp.float32
        )
        lowv = jnp.sum(masks[:, :, None] * down_proj, axis=0).astype(jnp.bfloat16)
        back_proj = jnp.einsum("rk,sdk->srd", lowu, down_local, preferred_element_type=jnp.float32)
        terms = (SCALE * jnp.sum(masks[:, :, None] * back_proj, axis=0)).astype(jnp.bfloat16)
        mask_bf = masks.astype(jnp.bfloat16)[:, :, None]
        masked_u = lowu[None] * mask_bf
        masked_v = lowv[None] * mask_bf
        add_down = SCALE * jnp.einsum(
            "rd,srk->sdk", input_sel, masked_u, preferred_element_type=jnp.float32
        )
        add_up = SCALE * jnp.einsum(
            "srk,rd->skd", masked_v, grad_sel, preferred_element_type=jnp.float32
        )
        acc_down = acc_down + jnp.where(valid, add_down, 0.0)
        acc_up = acc_up + jnp.where(valid, add_up, 0.0)
        returned = lax.all_to_all(terms, "dp", split_axis=1, concat_axis=0, tiled=True)
        frozen_part = lax.dot_general(
            grad_full, w_rows, (((1,), (1,)), ((), ())), preferred_element_type=jnp.float32
        )
        result = (
            frozen_part + jnp.dot(place, returned, preferred_element_type=jnp.float32)
        ).astype(jnp.bfloat16)
        updated = lax.dynamic_update_index_in_dim(in_grad, result, safe, 0)
        in_grad = jnp.where(valid, updated, in_grad)
        passed = passed_along(result, "section", -1)
        return (passed, acc_down, acc_up, in_grad)

    start = (
        jnp.zeros((tokens, columns), jnp.bfloat16),
        jnp.zeros((sen_local, width, rank), jnp.float32),
        jnp.zeros((sen_local, rank, width), jnp.float32),
        jnp.zeros((micro, tokens, columns), jnp.bfloat16),
    )
    received, acc_down, acc_up, in_grad = lax.fori_loop(0, micro + n_section - 1, step, start)
    weights = NORM_TOK / counts.astype(jnp.float32)
    scaled_down = acc_down * weights[:, None, None]
    scaled_up = acc_up * weights[:, None, None]
    local_sq = jnp.sum(scaled_down * scaled_down) + jnp.sum(scaled_up * scaled_up)
    total = lax.psum(local_sq, ("section", "dp"))
    limit = CLIP_RMS * math.sqrt(2.0 * n_section * n_dp * sen_local * width * rank)
    factor = jnp.minimum(1.0, limit / jnp.sqrt(total + 1e-06))
    return (
        in_grad[None],
        (scaled_down * factor).astype(jnp.bfloat16)[None],
        (scaled_up * factor).astype(jnp.bfloat16)[None],
    )


def solution(mesh):
    return jax.shard_map(
        per_device,
        mesh=mesh,
        in_specs=(
            P("section", "dp", None),
            P("section", "dp", None, None),
            P("section", "dp", None, None),
            P("section", None, None, "dp"),
            P(None, None, "dp"),
            P(),
            P("dp"),
        ),
        out_specs=(
            P("section", None, None, "dp"),
            P("section", "dp", None, None),
            P("section", "dp", None, None),
        ),
        check_vma=False,
    )
```

profile of v0, /device:TPU:0, one launch (start us, length us, event | category | flops | bytes accessed | tf_op | source)
XLA Modules:
  0.0 319.8 jit_solution(8361199157350096472)
XLA Ops:
  1.3 262.2 %while.24 = (s32[]{:T(128)}, bf16[24,1024]{1,0:T(8,128)(2,1)S(1)}, f32[2,8192,64]{1,2,0:T(8,128)}, f32[2,64,8192]{2,1,0:T(8,128)}, bf16[1,24,1024]{2,1,0:T(8,128...) while((s32[]{:T(128)}, bf16[24,1024]{1,0:T(8,128)(2,1)S(1)}, ...), condition=%wide.region_5.6_spmd.clone, body=%wide.region_0.5_spmd.clone.sunk | while | flops 481508608 | bytes 52930816 | solution.py:115
  2.5 0.8 bitcast_select_fusion.7
  3.3 16.2 %all_gather.26 = bf16[24,8192]{1,0:T(8,128)(2,1)S(1)} all-gather(bf16[24,1024]{1,0:T(8,128)(2,1)S(1)} %bitcast_select_fusion.7), channel_id=1, replica_groups=mesh['section'=4,'dp'=8] {'dp'}, dimensions={1}, use_global_device_ids=true | all-gather | bytes 442368 | tf_op jit(solution)/shard_map/while/body/eval_jaxpr/all_gather | solution.py:64
  20.1 2.5 fusion.97
  22.6 2.0 fusion.98
  25.3 4.7 %all-to-all-start = ((bf16[6,8,1024]{2,0,1:T(8,128)(2,1)}), bf16[6,8,1024]{2,0,1:T(8,128)(2,1)S(1)}, u32[]{:S(2)}, u32[]{:S(2)}) async-start(bf16[6,8,1024]{2,0,1:T(8,128)(2,1)} %bitcast.153), calls=%async_computation | async-start | bytes 262144 | tf_op jit(solution)/shard_map/while/body/eval_jaxpr/all_to_all | solution.py:97
  30.0 16.1 %all-gather.3 = bf16[1,24,8192]{2,1,0:T(8,128)(2,1)S(1)} all-gather(bf16[1,24,1024]{2,1,0:T(8,128)(2,1)S(1)} %copy-done.3), channel_id=2, replica_groups=mesh['section'=4,'dp'=8] {'dp'}, dimensions={2}, use_global_device_ids=true | all-gather | bytes 442368 | tf_op jit(solution)/shard_map/while/body/eval_jaxpr/all_gather | solution.py:65
  46.4 10.2 %fusion.93 = f32[24,1024]{1,0:T(8,128)S(1)} fusion(bf16[24,8192]{1,0:T(8,128)(2,1)S(1)} %all_gather.26, bf16[1024,8192]{1,0:T(8,128)(2,1)} %get-tuple-element.783), kind=kOutput, calls=%fused_computation.74.clone.1 | convolution fusion | flops 402653184 | bytes 17268736 | tf_op jit(solution)/shard_map/while/body/eval_jaxpr/dot_general | solution.py:98
  56.6 2.9 fusion.100
  59.5 0.9 fusion.101
  60.7 1.3 collective-permute-start
  62.0 2.9 fusion.102
  64.9 1.8 collective-permute-done
  68.6 14.6 %all_gather.26 = bf16[24,8192]{1,0:T(8,128)(2,1)S(1)} all-gather(bf16[24,1024]{1,0:T(8,128)(2,1)S(1)} %bitcast_select_fusion.7), channel_id=1, replica_groups=mesh['section'=4,'dp'=8] {'dp'}, dimensions={1}, use_global_device_ids=true | all-gather | bytes 442368 | tf_op jit(solution)/shard_map/while/body/eval_jaxpr/all_gather | solution.py:64
  83.7 2.5 fusion.97
  86.3 2.0 fusion.98
  88.9 3.4 %all-to-all-start = ((bf16[6,8,1024]{2,0,1:T(8,128)(2,1)}), bf16[6,8,1024]{2,0,1:T(8,128)(2,1)S(1)}, u32[]{:S(2)}, u32[]{:S(2)}) async-start(bf16[6,8,1024]{2,0,1:T(8,128)(2,1)} %bitcast.153), calls=%async_computation | async-start | bytes 262144 | tf_op jit(solution)/shard_map/while/body/eval_jaxpr/all_to_all | solution.py:97
  92.3 16.1 %all-gather.3 = bf16[1,24,8192]{2,1,0:T(8,128)(2,1)S(1)} all-gather(bf16[1,24,1024]{2,1,0:T(8,128)(2,1)S(1)} %copy-done.3), channel_id=2, replica_groups=mesh['section'=4,'dp'=8] {'dp'}, dimensions={2}, use_global_device_ids=true | all-gather | bytes 442368 | tf_op jit(solution)/shard_map/while/body/eval_jaxpr/all_gather | solution.py:65
  108.7 10.2 %fusion.93 = f32[24,1024]{1,0:T(8,128)S(1)} fusion(bf16[24,8192]{1,0:T(8,128)(2,1)S(1)} %all_gather.26, bf16[1024,8192]{1,0:T(8,128)(2,1)} %get-tuple-element.783), kind=kOutput, calls=%fused_computation.74.clone.1 | convolution fusion | flops 402653184 | bytes 17268736 | tf_op jit(solution)/shard_map/while/body/eval_jaxpr/dot_general | solution.py:98
  119.0 5.2 %fusion.100 = f32[2,8192,64]{1,2,0:T(8,128)} fusion(bf16[6,8192,1]{1,0,2:T(8,128)(2,1)S(1)} %fusion.99, f32[2,8192,64]{1,2,0:T(8,128)} %get-tuple-element.757, pred[]{:T(512)S(6)} %compare.48, pred[]{:T(512)S(6)} %and.133, bf16[2,6]{1,0:T(2,128)(2,1)S(1)} %get-tuple-element.732, bf16[6,64]{1,0:T(8,128)(2,1)S(1)} %fusion.97), kind=kOutput, calls=%fused_computation.4.clone.1 | convolution fusion | flops 16777984 | bytes 8487706 | tf_op jit(solution)/shard_map/while/body/eval_jaxpr/rd,srk->sdk/dot_general | solution.py:89
  124.2 0.9 fusion.101
  125.4 1.3 collective-permute-start
  126.7 5.1 %fusion.102 = f32[2,64,8192]{2,1,0:T(8,128)} fusion(bf16[6,8192,1]{1,0,2:T(8,128)(2,1)S(1)} %fusion.96, f32[2,64,8192]{2,1,0:T(8,128)} %get-tuple-element.758, pred[]{:T(512)S(6)} %compare.48, pred[]{:T(512)S(6)} %and.133, bf16[6,64]{1,0:T(8,128)(2,1)S(1)} %fusion.101, bf16[2,6]{1,0:T(2,128)(2,1)S(1)} %get-tuple-element.732), kind=kOutput, calls=%fused_computation.6.clone.1 | convolution fusion | flops 16777984 | bytes 8487706 | tf_op jit(solution)/shard_map/while/body/eval_jaxpr/srk,rd->skd/dot_general | solution.py:92
  133.9 14.4 %all_gather.26 = bf16[24,8192]{1,0:T(8,128)(2,1)S(1)} all-gather(bf16[24,1024]{1,0:T(8,128)(2,1)S(1)} %bitcast_select_fusion.7), channel_id=1, replica_groups=mesh['section'=4,'dp'=8] {'dp'}, dimensions={1}, use_global_device_ids=true | all-gather | bytes 442368 | tf_op jit(solution)/shard_map/while/body/eval_jaxpr/all_gather | solution.py:64
  148.9 2.5 fusion.97
  151.4 2.0 fusion.98
  154.1 3.6 %all-to-all-start = ((bf16[6,8,1024]{2,0,1:T(8,128)(2,1)}), bf16[6,8,1024]{2,0,1:T(8,128)(2,1)S(1)}, u32[]{:S(2)}, u32[]{:S(2)}) async-start(bf16[6,8,1024]{2,0,1:T(8,128)(2,1)} %bitcast.153), calls=%async_computation | async-start | bytes 262144 | tf_op jit(solution)/shard_map/while/body/eval_jaxpr/all_to_all | solution.py:97
  157.7 16.1 %all-gather.3 = bf16[1,24,8192]{2,1,0:T(8,128)(2,1)S(1)} all-gather(bf16[1,24,1024]{2,1,0:T(8,128)(2,1)S(1)} %copy-done.3), channel_id=2, replica_groups=mesh['section'=4,'dp'=8] {'dp'}, dimensions={2}, use_global_device_ids=true | all-gather | bytes 442368 | tf_op jit(solution)/shard_map/while/body/eval_jaxpr/all_gather | solution.py:65
  174.1 10.2 %fusion.93 = f32[24,1024]{1,0:T(8,128)S(1)} fusion(bf16[24,8192]{1,0:T(8,128)(2,1)S(1)} %all_gather.26, bf16[1024,8192]{1,0:T(8,128)(2,1)} %get-tuple-element.783), kind=kOutput, calls=%fused_computation.74.clone.1 | convolution fusion | flops 402653184 | bytes 17268736 | tf_op jit(solution)/shard_map/while/body/eval_jaxpr/dot_general | solution.py:98
  184.3 5.2 %fusion.100 = f32[2,8192,64]{1,2,0:T(8,128)} fusion(bf16[6,8192,1]{1,0,2:T(8,128)(2,1)S(1)} %fusion.99, f32[2,8192,64]{1,2,0:T(8,128)} %get-tuple-element.757, pred[]{:T(512)S(6)} %compare.48, pred[]{:T(512)S(6)} %and.133, bf16[2,6]{1,0:T(2,128)(2,1)S(1)} %get-tuple-element.732, bf16[6,64]{1,0:T(8,128)(2,1)S(1)} %fusion.97), kind=kOutput, calls=%fused_computation.4.clone.1 | convolution fusion | flops 16777984 | bytes 8487706 | tf_op jit(solution)/shard_map/while/body/eval_jaxpr/rd,srk->sdk/dot_general | solution.py:89
  189.5 0.9 fusion.101
  190.7 1.3 collective-permute-start
  192.0 5.1 %fusion.102 = f32[2,64,8192]{2,1,0:T(8,128)} fusion(bf16[6,8192,1]{1,0,2:T(8,128)(2,1)S(1)} %fusion.96, f32[2,64,8192]{2,1,0:T(8,128)} %get-tuple-element.758, pred[]{:T(512)S(6)} %compare.48, pred[]{:T(512)S(6)} %and.133, bf16[6,64]{1,0:T(8,128)(2,1)S(1)} %fusion.101, bf16[2,6]{1,0:T(2,128)(2,1)S(1)} %get-tuple-element.732), kind=kOutput, calls=%fused_computation.6.clone.1 | convolution fusion | flops 16777984 | bytes 8487706 | tf_op jit(solution)/shard_map/while/body/eval_jaxpr/srk,rd->skd/dot_general | solution.py:92
  199.7 14.4 %all_gather.26 = bf16[24,8192]{1,0:T(8,128)(2,1)S(1)} all-gather(bf16[24,1024]{1,0:T(8,128)(2,1)S(1)} %bitcast_select_fusion.7), channel_id=1, replica_groups=mesh['section'=4,'dp'=8] {'dp'}, dimensions={1}, use_global_device_ids=true | all-gather | bytes 442368 | tf_op jit(solution)/shard_map/while/body/eval_jaxpr/all_gather | solution.py:64
  214.6 2.5 fusion.97
  217.2 2.0 fusion.98
  219.8 3.5 %all-to-all-start = ((bf16[6,8,1024]{2,0,1:T(8,128)(2,1)}), bf16[6,8,1024]{2,0,1:T(8,128)(2,1)S(1)}, u32[]{:S(2)}, u32[]{:S(2)}) async-start(bf16[6,8,1024]{2,0,1:T(8,128)(2,1)} %bitcast.153), calls=%async_computation | async-start | bytes 262144 | tf_op jit(solution)/shard_map/while/body/eval_jaxpr/all_to_all | solution.py:97
  223.4 16.1 %all-gather.3 = bf16[1,24,8192]{2,1,0:T(8,128)(2,1)S(1)} all-gather(bf16[1,24,1024]{2,1,0:T(8,128)(2,1)S(1)} %copy-done.3), channel_id=2, replica_groups=mesh['section'=4,'dp'=8] {'dp'}, dimensions={2}, use_global_device_ids=true | all-gather | bytes 442368 | tf_op jit(solution)/shard_map/while/body/eval_jaxpr/all_gather | solution.py:65
  239.8 10.2 %fusion.93 = f32[24,1024]{1,0:T(8,128)S(1)} fusion(bf16[24,8192]{1,0:T(8,128)(2,1)S(1)} %all_gather.26, bf16[1024,8192]{1,0:T(8,128)(2,1)} %get-tuple-element.783), kind=kOutput, calls=%fused_computation.74.clone.1 | convolution fusion | flops 402653184 | bytes 17268736 | tf_op jit(solution)/shard_map/while/body/eval_jaxpr/dot_general | solution.py:98
  250.0 5.2 %fusion.100 = f32[2,8192,64]{1,2,0:T(8,128)} fusion(bf16[6,8192,1]{1,0,2:T(8,128)(2,1)S(1)} %fusion.99, f32[2,8192,64]{1,2,0:T(8,128)} %get-tuple-element.757, pred[]{:T(512)S(6)} %compare.48, pred[]{:T(512)S(6)} %and.133, bf16[2,6]{1,0:T(2,128)(2,1)S(1)} %get-tuple-element.732, bf16[6,64]{1,0:T(8,128)(2,1)S(1)} %fusion.97), kind=kOutput, calls=%fused_computation.4.clone.1 | convolution fusion | flops 16777984 | bytes 8487706 | tf_op jit(solution)/shard_map/while/body/eval_jaxpr/rd,srk->sdk/dot_general | solution.py:89
  255.2 0.9 fusion.101
  256.4 1.3 collective-permute-start
  257.7 5.1 %fusion.102 = f32[2,64,8192]{2,1,0:T(8,128)} fusion(bf16[6,8192,1]{1,0,2:T(8,128)(2,1)S(1)} %fusion.96, f32[2,64,8192]{2,1,0:T(8,128)} %get-tuple-element.758, pred[]{:T(512)S(6)} %compare.48, pred[]{:T(512)S(6)} %and.133, bf16[6,64]{1,0:T(8,128)(2,1)S(1)} %fusion.101, bf16[2,6]{1,0:T(2,128)(2,1)S(1)} %get-tuple-element.732), kind=kOutput, calls=%fused_computation.6.clone.1 | convolution fusion | flops 16777984 | bytes 8487706 | tf_op jit(solution)/shard_map/while/body/eval_jaxpr/srk,rd->skd/dot_general | solution.py:92
  263.5 4.1 %multiply_reduce_fusion = f32[]{:T(128)} fusion(f32[2,64,8192]{2,1,0:T(8,128)} %get-tuple-element.494, f32[2]{0:T(128)S(1)} %convert_divide_fusion), kind=kLoop, calls=%fused_computation.65 | loop fusion | flops 3145727 | bytes 4194316 | tf_op jit(solution)/shard_map/reduce_sum | solution.py:119
  267.6 1.8 multiply_reduce_fusion.1
  270.8 42.4 %psum.7 = f32[]{:T(128)} all-reduce(f32[]{:T(128)S(6)} %add.192), channel_id=1, replica_groups=mesh['section'=4,'dp'=8] {'section','dp'}, use_global_device_ids=true, to_apply=%region_8.9 | all-reduce | flops 1 | bytes 8 | tf_op jit(solution)/shard_map/psum | solution.py:120
  313.8 4.2 %fusion.35 = bf16[1,2,64,8192]{3,2,1,0:T(8,128)(2,1)} fusion(f32[2,64,8192]{2,1,0:T(8,128)} %get-tuple-element.494, f32[]{:T(128)S(6)} %min_shard_map.3, f32[2]{0:T(128)S(1)} %convert_divide_fusion), kind=kLoop, calls=%fused_computation.68 | loop fusion | flops 3145728 | bytes 6291468 | tf_op jit(solution)/shard_map/broadcast_in_dim | solution.py:126
  318.0 1.8 fusion.34
  (96 shorter events, 16.5 us)
Async XLA Ops:
  1.3 262.2 %copy-start.5 = (s32[2]{0:T(128)S(1)}, s32[2]{0:T(128)}, u32[]{:S(2)}) copy-start(s32[2]{0:T(128)} %param.15) | copy-start | bytes 28
  1.3 28.6 %copy-start.3 = (bf16[1,24,1024]{2,1,0:T(8,128)(2,1)S(1)}, bf16[1,24,1024]{2,1,0:T(8,128)(2,1)}, u32[]{:S(2)}) copy-start(bf16[1,24,1024]{2,1,0:T(8,128)(2,1)} %get-tuple-element.794) | copy-start | bytes 147460 | tf_op jit(solution)/shard_map/while
  25.3 35.1 %all-to-all-start = ((bf16[6,8,1024]{2,0,1:T(8,128)(2,1)}), bf16[6,8,1024]{2,0,1:T(8,128)(2,1)S(1)}, u32[]{:S(2)}, u32[]{:S(2)}) async-start(bf16[6,8,1024]{2,0,1:T(8,128)(2,1)} %bitcast.153), calls=%async_computation | async-start | bytes 262144 | tf_op jit(solution)/shard_map/while/body/eval_jaxpr/all_to_all | solution.py:97
  56.6 2.9 copy-start
  60.7 6.0 %collective-permute-start = (bf16[24,1024]{1,0:T(8,128)(2,1)S(1)}, bf16[24,1024]{1,0:T(8,128)(2,1)S(1)}, u32[]{:S(2)}, u32[]{:S(2)}) collective-permute-start(bf16[24,1024]{1,0:T(8,128)(2,1)S(1)} %get-tuple-element.731), channel_id=1, source_target_pairs={{8,0},{16,8},{24,16},{9,1},{17,9},{25,17},{10,2},{18,10},{26,18},{... | collective-permute-start | bytes 147464 | tf_op jit(solution)/shard_map/while/body/eval_jaxpr/ppermute | solution.py:19
  66.7 25.7 %copy-start.3 = (bf16[1,24,1024]{2,1,0:T(8,128)(2,1)S(1)}, bf16[1,24,1024]{2,1,0:T(8,128)(2,1)}, u32[]{:S(2)}) copy-start(bf16[1,24,1024]{2,1,0:T(8,128)(2,1)} %get-tuple-element.794) | copy-start | bytes 147460 | tf_op jit(solution)/shard_map/while
  88.9 36.1 %all-to-all-start = ((bf16[6,8,1024]{2,0,1:T(8,128)(2,1)}), bf16[6,8,1024]{2,0,1:T(8,128)(2,1)S(1)}, u32[]{:S(2)}, u32[]{:S(2)}) async-start(bf16[6,8,1024]{2,0,1:T(8,128)(2,1)} %bitcast.153), calls=%async_computation | async-start | bytes 262144 | tf_op jit(solution)/shard_map/while/body/eval_jaxpr/all_to_all | solution.py:97
  119.0 5.2 %copy-start = (bf16[2,8192,64]{1,2,0:T(8,128)(2,1)S(1)}, bf16[2,8192,64]{1,2,0:T(8,128)(2,1)}, u32[]{:S(2)}) copy-start(bf16[2,8192,64]{1,2,0:T(8,128)(2,1)} %get-tuple-element.792) | copy-start | bytes 6291460 | tf_op jit(solution)/shard_map/while
  125.4 6.5 %collective-permute-start = (bf16[24,1024]{1,0:T(8,128)(2,1)S(1)}, bf16[24,1024]{1,0:T(8,128)(2,1)S(1)}, u32[]{:S(2)}, u32[]{:S(2)}) collective-permute-start(bf16[24,1024]{1,0:T(8,128)(2,1)S(1)} %get-tuple-element.731), channel_id=1, source_target_pairs={{8,0},{16,8},{24,16},{9,1},{17,9},{25,17},{10,2},{18,10},{26,18},{... | collective-permute-start | bytes 147464 | tf_op jit(solution)/shard_map/while/body/eval_jaxpr/ppermute | solution.py:19
  131.9 25.8 %copy-start.3 = (bf16[1,24,1024]{2,1,0:T(8,128)(2,1)S(1)}, bf16[1,24,1024]{2,1,0:T(8,128)(2,1)}, u32[]{:S(2)}) copy-start(bf16[1,24,1024]{2,1,0:T(8,128)(2,1)} %get-tuple-element.794) | copy-start | bytes 147460 | tf_op jit(solution)/shard_map/while
  154.1 36.4 %all-to-all-start = ((bf16[6,8,1024]{2,0,1:T(8,128)(2,1)}), bf16[6,8,1024]{2,0,1:T(8,128)(2,1)S(1)}, u32[]{:S(2)}, u32[]{:S(2)}) async-start(bf16[6,8,1024]{2,0,1:T(8,128)(2,1)} %bitcast.153), calls=%async_computation | async-start | bytes 262144 | tf_op jit(solution)/shard_map/while/body/eval_jaxpr/all_to_all | solution.py:97
  184.3 5.2 %copy-start = (bf16[2,8192,64]{1,2,0:T(8,128)(2,1)S(1)}, bf16[2,8192,64]{1,2,0:T(8,128)(2,1)}, u32[]{:S(2)}) copy-start(bf16[2,8192,64]{1,2,0:T(8,128)(2,1)} %get-tuple-element.792) | copy-start | bytes 6291460 | tf_op jit(solution)/shard_map/while
  190.7 7.0 %collective-permute-start = (bf16[24,1024]{1,0:T(8,128)(2,1)S(1)}, bf16[24,1024]{1,0:T(8,128)(2,1)S(1)}, u32[]{:S(2)}, u32[]{:S(2)}) collective-permute-start(bf16[24,1024]{1,0:T(8,128)(2,1)S(1)} %get-tuple-element.731), channel_id=1, source_target_pairs={{8,0},{16,8},{24,16},{9,1},{17,9},{25,17},{10,2},{18,10},{26,18},{... | collective-permute-start | bytes 147464 | tf_op jit(solution)/shard_map/while/body/eval_jaxpr/ppermute | solution.py:19
  197.7 25.7 %copy-start.3 = (bf16[1,24,1024]{2,1,0:T(8,128)(2,1)S(1)}, bf16[1,24,1024]{2,1,0:T(8,128)(2,1)}, u32[]{:S(2)}) copy-start(bf16[1,24,1024]{2,1,0:T(8,128)(2,1)} %get-tuple-element.794) | copy-start | bytes 147460 | tf_op jit(solution)/shard_map/while
  219.8 36.3 %all-to-all-start = ((bf16[6,8,1024]{2,0,1:T(8,128)(2,1)}), bf16[6,8,1024]{2,0,1:T(8,128)(2,1)S(1)}, u32[]{:S(2)}, u32[]{:S(2)}) async-start(bf16[6,8,1024]{2,0,1:T(8,128)(2,1)} %bitcast.153), calls=%async_computation | async-start | bytes 262144 | tf_op jit(solution)/shard_map/while/body/eval_jaxpr/all_to_all | solution.py:97
  250.0 5.2 %copy-start = (bf16[2,8192,64]{1,2,0:T(8,128)(2,1)S(1)}, bf16[2,8192,64]{1,2,0:T(8,128)(2,1)}, u32[]{:S(2)}) copy-start(bf16[2,8192,64]{1,2,0:T(8,128)(2,1)} %get-tuple-element.792) | copy-start | bytes 6291460 | tf_op jit(solution)/shard_map/while
  256.4 7.1 %collective-permute-start = (bf16[24,1024]{1,0:T(8,128)(2,1)S(1)}, bf16[24,1024]{1,0:T(8,128)(2,1)S(1)}, u32[]{:S(2)}, u32[]{:S(2)}) collective-permute-start(bf16[24,1024]{1,0:T(8,128)(2,1)S(1)} %get-tuple-element.731), channel_id=1, source_target_pairs={{8,0},{16,8},{24,16},{9,1},{17,9},{25,17},{10,2},{18,10},{26,18},{... | collective-permute-start | bytes 147464 | tf_op jit(solution)/shard_map/while/body/eval_jaxpr/ppermute | solution.py:19
  263.5 6.0 %copy-start.4 = (bf16[1,24,1024]{2,1,0:T(8,128)(2,1)}, bf16[1,24,1024]{2,1,0:T(8,128)(2,1)S(1)}, u32[]{:S(2)}) copy-start(bf16[1,24,1024]{2,1,0:T(8,128)(2,1)S(1)} %get-tuple-element.492) | copy-start | bytes 147460
  263.5 4.1 %copy-start.1 = (f32[2,8192,64]{1,2,0:T(8,128)S(1)}, f32[2,8192,64]{1,2,0:T(8,128)}, u32[]{:S(2)}) copy-start(f32[2,8192,64]{1,2,0:T(8,128)} %get-tuple-element.493) | copy-start | bytes 12582916
  313.8 4.2 %copy-start.2 = (f32[2,8192,64]{1,2,0:T(8,128)S(1)}, f32[2,8192,64]{1,2,0:T(8,128)}, u32[]{:S(2)}) copy-start(f32[2,8192,64]{1,2,0:T(8,128)} %get-tuple-element.493) | copy-start | bytes 12582916
where the time goes:
time: 321 us; the launch traced here: 320 us
  blocking collectives  166 us (52%)
  matrix products  103 us (32%)
  other arithmetic  22.2 us (7%)
  starting transfers between devices  20.3 us (6%)
  waiting for transfers between devices  3.35 us (1%)
    all_gather x4, blocking collectives, step(): lax.all_gather(inputs_cols, 'dp', axis=1, tiled=True)  64.4 us
    all_gather x4, blocking collectives, step(): lax.all_gather(current, 'dp', axis=1, tiled=True)  59.6 us
    psum x1, blocking collectives, per_device(): total = lax.psum(local_sq, ('section', 'dp'))  42.4 us
    dot_general x4, matrix products, step(): lax.dot_general(grad_full, w_rows, (((1,), (1,)), ((), ())), preferred_el...  40.9 us
    dot_general x4, matrix products, step(): jnp.einsum('rd,srk->sdk', input_sel, masked_u, preferred_element_type=jnp...  18.4 us
    dot_general x4, matrix products, step(): jnp.einsum('srk,rd->skd', masked_v, grad_sel, preferred_element_type=jnp....  18.1 us
    all_to_all x4, starting transfers between devices, step(): lax.all_to_all(terms, 'dp', split_axis=1, concat_axis=0, tiled=True)  15.2 us
    dot_general x4, matrix products, step(): jnp.einsum('rd,skd->srk', grad_sel, up_local, preferred_element_type=jnp....  10 us
  transfers between devices with their start and end apart: 8, of which 4 were waited for; matrix products, arithmetic and copies ran while one was open for 26% of the time, Pallas kernels for 0%

commit v1 on v0

v1 whole, which is shorter than its diff:
```python
import functools
import math

import jax
import jax.numpy as jnp
from jax import lax
from jax.experimental import pallas as pl
from jax.experimental.pallas import tpu as pltpu
from jax.sharding import PartitionSpec as P

CAP = 2
SCALE = 2.0
NORM_TOK = 1024.0
CLIP_RMS = 0.5
MESH = pl.DeviceIdType.MESH
SLOT = 16


def mm_t(a, b):
    return lax.dot_general(a, b, (((1,), (1,)), ((), ())), preferred_element_type=jnp.float32)


def mm(a, b):
    return jnp.dot(a, b, preferred_element_type=jnp.float32)


def chain_kernel(
    n_sec, n_dp, rank, pack, limit,
    w_hbm, dn_hbm, up_hbm, x_in, g_in, sens_col, tgt_col, tgt_row, w2_col,
    res_out, x_out, g_out, u_out, v_out, fac_out,
    wbuf, dbuf, ubuf, xbuf, gbuf, lsend, lrecv, acc, uacc, vacc, gram_x, chain_in, chain_out, norms,
    w_sem, a_sem, o_sem, x_rs, x_ss, x_fs, g_rs, og_ss, g_ss, g_fs, l_ss, l_rs, c_ss, c_rs, n_ss, n_rs,
):
    sec = lax.axis_index("section")
    me = lax.axis_index("dp")
    par = lax.rem(me, 2)
    partner = me + 1 - 2 * par
    half = n_dp // 2
    my = me // 2
    way = 1 - 2 * (my // max(half // 2, 1))
    top = n_sec - 1
    is_top = sec == top
    tokens, columns = x_in.shape
    rows = xbuf.shape[1]
    wide = columns // pack
    lanes = uacc.shape[1]

    def near(k):
        return lax.rem(my + way * k + half, half)

    def cols(j):
        return pl.ds(pl.multiple_of(j * columns, columns), columns)

    def w_copy(j):
        return pltpu.make_async_copy(w_hbm.at[:, cols(j)], wbuf.at[:, cols(j)], w_sem.at[j])

    up_copy = pltpu.make_async_copy(up_hbm, ubuf, a_sem.at[0])
    dn_copy = pltpu.make_async_copy(dn_hbm, dbuf, a_sem.at[1])
    up_copy.start()
    dn_copy.start()

    def start_w(k, carry):
        w_copy(2 * near(k) + par).start()
        return carry

    def start_w_other(k, carry):
        w_copy(2 * near(k) + 1 - par).start()
        return carry

    lax.fori_loop(0, half, start_w, 0)
    lax.fori_loop(0, half, start_w_other, 0)

    barrier = pltpu.get_barrier_semaphore()
    for q in range(n_sec):
        def greet(d, carry, q=q):
            @pl.when((sec != q) | (me != d))
            def _():
                pl.semaphore_signal(barrier, inc=1, device_id=(q, d), device_id_type=MESH)
            return carry
        lax.fori_loop(0, n_dp, greet, 0)

    def padded(ref):
        value = ref[...]
        if rows == tokens:
            return value
        tail = jnp.zeros((rows - tokens, columns), jnp.float32)
        return jnp.concatenate([value.astype(jnp.float32), tail], axis=0).astype(jnp.bfloat16)

    xbuf[me] = padded(x_in)

    @pl.when(is_top)
    def _():
        gbuf[me] = padded(g_in)

    pl.semaphore_wait(barrier, n_sec * n_dp - 1)

    def remote(src, dst, ss, rs, q, d):
        return pltpu.make_async_remote_copy(
            src_ref=src, dst_ref=dst, send_sem=ss, recv_sem=rs, device_id=(q, d), device_id_type=MESH
        )

    def og_copy(k):
        return remote(gbuf.at[me], gbuf.at[me], og_ss.at[k], g_rs.at[me], sec, 2 * near(k) + par)

    def x_copy(k):
        return remote(xbuf.at[me], xbuf.at[me], x_ss.at[k], x_rs.at[me], sec, 2 * near(k) + par)

    def x_forward(j):
        return remote(xbuf.at[j], xbuf.at[j], x_fs.at[j // 2], x_rs.at[j], sec, partner)

    def g_forward(j):
        return remote(gbuf.at[j], gbuf.at[j], g_fs.at[j // 2], g_rs.at[j], sec, partner)

    def res_copy(k):
        return remote(res_out, gbuf.at[me], g_ss.at[k], g_rs.at[me], sec - 1, 2 * near(k) + par)

    def low_copy(j):
        return remote(lsend.at[j], lrecv.at[me], l_ss.at[j], l_rs.at[me], sec, j)

    def low_arrival(j):
        return remote(lsend.at[j], lrecv.at[j], l_ss.at[j], l_rs.at[j], sec, partner)

    def loop(lo, hi, body):
        def step(k, carry):
            body(k)
            return carry
        lax.fori_loop(lo, hi, step, 0)

    lane_sensor = lax.broadcasted_iota(jnp.int32, (rows, lanes), 1) // rank
    own = sens_col[...] == me * (lanes // rank) + lane_sensor

    def x_work():
        loop(1, half, lambda k: x_copy(k).start())
        vacc[...] = jnp.zeros_like(vacc)
        gram_x[...] = jnp.zeros_like(gram_x)

        def use(j):
            piece = xbuf[j]
            vacc[...] += mm_t(piece, dbuf[:, cols(j)])
            gram_x[...] += mm_t(piece, piece)

        def first(k):
            j = 2 * near(k) + par

            @pl.when(k > 0)
            def _():
                x_forward(j).wait_recv()
            x_forward(j).start()
            use(j)

        def second(k):
            j = 2 * near(k) + 1 - par
            x_forward(j).wait_recv()
            use(j)

        loop(0, half, first)
        loop(0, half, second)
        v_out[...] = jnp.where(own, vacc[...], 0.0).astype(jnp.bfloat16)
        pltpu.make_async_copy(xbuf, x_out, o_sem.at[0]).start()

    @pl.when(is_top)
    def _():
        loop(1, half, lambda k: og_copy(k).start())

    dn_copy.wait()
    up_copy.wait()

    @pl.when(sec != top)
    def _():
        x_work()

    acc[...] = jnp.zeros_like(acc)
    uacc[...] = jnp.zeros_like(uacc)

    def g_first(k):
        j = 2 * near(k) + par

        @pl.when((k > 0) | (sec != top))
        def _():
            g_forward(j).wait_recv()
        g_forward(j).start()
        w_copy(j).wait()
        piece = gbuf[j]
        uacc[...] += mm_t(piece, ubuf[:, cols(j)])
        acc[...] += mm_t(piece, wbuf[:, cols(j)])

    def g_second(k):
        j = 2 * near(k) + 1 - par
        g_forward(j).wait_recv()
        uacc[...] += mm_t(gbuf[j], ubuf[:, cols(j)])

    loop(0, half, g_first)
    loop(0, half, g_second)
    u_out[...] = jnp.where(own, uacc[...], 0.0).astype(jnp.bfloat16)

    slot_at = lax.broadcasted_iota(jnp.int32, (SLOT, rows), 0) + me * SLOT
    in_slot = lax.broadcasted_iota(jnp.int32, (SLOT, rows), 0) < SLOT // pack
    select = jnp.where((tgt_row[...] == slot_at) & in_slot, 1.0, 0.0).astype(jnp.bfloat16)
    u_sel = mm(select, u_out[...]).astype(jnp.bfloat16)

    def low_work(k):
        j = lax.rem(me + k, n_dp)
        low = SCALE * mm(u_sel, dbuf[:, cols(j)])
        if pack == 2:
            low = jnp.concatenate([low[: SLOT // 2, :wide], low[: SLOT // 2, wide:]], axis=0)
        low = low.astype(jnp.bfloat16)

        @pl.when(k < n_dp)
        def _():
            lsend[j] = low
            low_copy(j).start()

        @pl.when(k == n_dp)
        def _():
            lrecv[me] = low

    loop(1, n_dp + 1, low_work)

    def chain_copy():
        return remote(chain_out, chain_in, c_ss, c_rs, sec - 1, me)

    def norm_copy(q, d):
        return remote(norms.at[me], norms.at[me], n_ss.at[q, d], n_rs.at[me], q, d)

    def norm_value():
        def add(j, total):
            piece = gbuf[j]
            return total + mm_t(piece, piece)
        gram_g = lax.fori_loop(0, n_dp, add, jnp.zeros((rows, rows), jnp.float32))
        uu = mm_t(u_out[...], u_out[...])
        vv = mm_t(v_out[...], v_out[...])
        whole = jnp.sum((gram_x[...] * uu + gram_g * vv) * w2_col[...], axis=0, keepdims=True)
        return jnp.broadcast_to(jnp.sum(whole, axis=1, keepdims=True), (1, 128))

    @pl.when(sec == 0)
    def _():
        value = norm_value()
        chain_copy().wait_recv()
        norms[me] = value + chain_in[...]
        for q in range(n_sec):
            def send(d, q=q):
                @pl.when((me != d) | (q != 0))
                def _():
                    norm_copy(q, d).start()
            loop(0, n_dp, send)

    def g_third(k):
        j = 2 * near(k) + 1 - par
        w_copy(j).wait()
        acc[...] += mm_t(gbuf[j], wbuf[:, cols(j)])

    loop(0, half, g_third)

    def low_wait(j):
        @pl.when(j != me)
        def _():
            low_arrival(j).wait_recv()

    loop(0, n_dp, low_wait)
    terms = lrecv[...].reshape(n_dp * SLOT, wide)
    lane_at = lax.broadcasted_iota(jnp.int32, (rows, n_dp * SLOT), 1)
    parts = []
    for h in range(pack):
        place = jnp.where(tgt_col[...] + h * (SLOT // 2) == lane_at, 1.0, 0.0).astype(jnp.bfloat16)
        parts.append(acc[:, h * wide : (h + 1) * wide] + mm(place, terms))
    res_out[...] = (parts[0] if pack == 1 else jnp.concatenate(parts, axis=1)).astype(jnp.bfloat16)

    @pl.when(sec > 0)
    def _():
        loop(0, half, lambda k: res_copy(k).start())

    pltpu.make_async_copy(gbuf, g_out, o_sem.at[1]).start()

    @pl.when(is_top)
    def _():
        x_work()

    @pl.when(sec > 0)
    def _():
        value = norm_value()

        @pl.when(is_top)
        def _():
            chain_out[...] = value

        @pl.when(sec != top)
        def _():
            chain_copy().wait_recv()
            chain_out[...] = value + chain_in[...]
        chain_copy().start()

    def norm_wait(j):
        @pl.when((sec != 0) | (me != j))
        def _():
            remote(norms.at[j], norms.at[j], n_ss.at[0, j], n_rs.at[j], 0, partner).wait_recv()

    @pl.when(is_top)
    def _():
        loop(1, half, lambda k: og_copy(k).wait_send())

    @pl.when(sec > 0)
    def _():
        loop(0, half, lambda k: res_copy(k).wait_send())
        chain_copy().wait_send()

    loop(1, half, lambda k: x_copy(k).wait_send())
    loop(0, half, lambda k: x_forward(2 * near(k) + par).wait_send())
    loop(0, half, lambda k: g_forward(2 * near(k) + par).wait_send())

    def low_sent(j):
        @pl.when(j != me)
        def _():
            low_copy(j).wait_send()

    loop(0, n_dp, low_sent)
    pltpu.make_async_copy(xbuf, x_out, o_sem.at[0]).wait()
    pltpu.make_async_copy(gbuf, g_out, o_sem.at[1]).wait()

    loop(0, n_dp, norm_wait)
    total = jnp.maximum(jnp.sum(norms[...], axis=0), 0.0)
    fac_out[...] = jnp.minimum(1.0, limit / jnp.sqrt(total + 1e-06))

    @pl.when(sec == 0)
    def _():
        for q in range(n_sec):
            def sent(d, q=q):
                @pl.when((me != d) | (q != 0))
                def _():
                    norm_copy(q, d).wait_send()
            loop(0, n_dp, sent)


def write_kernel(x_ref, g_ref, u_ref, v_ref, fac_ref, scale_ref, down_ref, up_ref):
    scale = scale_ref[...] * fac_ref[0:1, 0:1]
    tn = (((0,), (0,)), ((), ()))
    down = lax.dot_general(u_ref[...], x_ref[0], tn, preferred_element_type=jnp.float32)
    down_ref[...] = (down * scale).astype(jnp.bfloat16)
    up = lax.dot_general(v_ref[...], g_ref[0], tn, preferred_element_type=jnp.float32)
    up_ref[...] = (up * scale).astype(jnp.bfloat16)


def per_device(n_sec, n_dp, frozen, adapt_down, adapt_up, saved_inputs, out_grad, sensor, counts):
    me = lax.axis_index("dp")
    tokens, columns = out_grad.shape[1:]
    width = columns * n_dp
    blocks = sensor.shape[1]
    block_rows = tokens // blocks
    sen_local, rank = adapt_up.shape[1:3]
    lanes = sen_local * rank
    rows = -(-tokens // 16) * 16
    pack = 2 if columns % 256 == 0 else 1
    w_rows = frozen.shape[1]

    idents = sensor[0]
    owners = idents // sen_local
    order = jnp.arange(blocks, dtype=jnp.int32)
    earlier = (owners[:, None] == owners[None, :]) & (order[:, None] < order[None, :])
    position = jnp.sum(earlier.astype(jnp.int32), axis=0)
    first = owners * SLOT + position * block_rows
    target = (first[:, None] + jnp.arange(block_rows, dtype=jnp.int32)[None, :]).reshape(-1)
    more = (0, rows - tokens)
    target = jnp.pad(target, more, constant_values=-SLOT)
    sens = jnp.pad(jnp.repeat(idents, block_rows), more, constant_values=-1)
    weights = SCALE * (NORM_TOK / counts.astype(jnp.float32))
    held = sens[:, None] == me * sen_local + jnp.arange(sen_local, dtype=jnp.int32)[None, :]
    w2 = jnp.sum(jnp.where(held, (weights * weights)[None, :], 0.0), axis=1)
    scale_col = jnp.repeat(weights, rank)[:, None]
    limit = CLIP_RMS * math.sqrt(2.0 * n_sec * n_dp * sen_local * width * rank)

    bf, f32 = jnp.bfloat16, jnp.float32
    vm = pl.BlockSpec(memory_space=pltpu.VMEM)
    anywhere = pl.BlockSpec(memory_space=pl.ANY)
    half = n_dp // 2
    dma = pltpu.SemaphoreType.DMA
    result, x_full, g_full, u, v, factor = pl.pallas_call(
        functools.partial(chain_kernel, n_sec, n_dp, rank, pack, limit),
        out_shape=(
            jax.ShapeDtypeStruct((rows, columns), bf),
            jax.ShapeDtypeStruct((n_dp, rows, columns), bf),
            jax.ShapeDtypeStruct((n_dp, rows, columns), bf),
            jax.ShapeDtypeStruct((rows, lanes), bf),
            jax.ShapeDtypeStruct((rows, lanes), bf),
            jax.ShapeDtypeStruct((1, 128), f32),
        ),
        in_specs=[anywhere] * 3 + [vm] * 6,
        out_specs=(vm, anywhere, anywhere, vm, vm, vm),
        scratch_shapes=[
            pltpu.VMEM((w_rows, width), bf),
            pltpu.VMEM((lanes, width), bf),
            pltpu.VMEM((lanes, width), bf),
            pltpu.VMEM((n_dp, rows, columns), bf),
            pltpu.VMEM((n_dp, rows, columns), bf),
            pltpu.VMEM((n_dp, SLOT, columns // pack), bf),
            pltpu.VMEM((n_dp, SLOT, columns // pack), bf),
            pltpu.VMEM((rows, columns), f32),
            pltpu.VMEM((rows, lanes), f32),
            pltpu.VMEM((rows, lanes), f32),
            pltpu.VMEM((rows, rows), f32),
            pltpu.VMEM((1, 128), f32),
            pltpu.VMEM((1, 128), f32),
            pltpu.VMEM((n_dp, 1, 128), f32),
            dma((n_dp,)),
            dma((2,)),
            dma((2,)),
            dma((n_dp,)),
            dma((half,)),
            dma((half,)),
            dma((n_dp,)),
            dma((half,)),
            dma((half,)),
            dma((half,)),
            dma((n_dp,)),
            dma((n_dp,)),
            dma,
            dma,
            dma((n_sec, n_dp)),
            dma((n_dp,)),
        ],
        compiler_params=pltpu.CompilerParams(
            collective_id=0, has_side_effects=True, vmem_limit_bytes=48 * 1024 * 1024
        ),
        name="chain",
    )(
        frozen[0],
        jnp.swapaxes(adapt_down[0], 1, 2).reshape(lanes, width),
        adapt_up[0].reshape(lanes, width),
        saved_inputs[0, 0],
        out_grad[0],
        sens[:, None],
        target[:, None],
        target[None, :],
        w2[:, None],
    )

    fixed = lambda shape: pl.BlockSpec(shape, lambda j: (0, 0))
    piece = pl.BlockSpec((1, rows, columns), lambda j: (j, 0, 0))
    grown = pl.BlockSpec((lanes, columns), lambda j: (0, j))
    down, up = pl.pallas_call(
        write_kernel,
        grid=(n_dp,),
        out_shape=(jax.ShapeDtypeStruct((lanes, width), bf),) * 2,
        in_specs=[piece, piece, fixed((rows, lanes)), fixed((rows, lanes)), fixed((1, 128)), fixed((lanes, 1))],
        out_specs=(grown, grown),
        name="write",
    )(x_full, g_full, u, v, factor, scale_col)
    return (
        result[:tokens][None, None],
        jnp.swapaxes(down.reshape(sen_local, rank, width), 1, 2)[None],
        up.reshape(sen_local, rank, width)[None],
    )


def solution(mesh):
    return jax.shard_map(
        functools.partial(per_device, mesh.shape["section"], mesh.shape["dp"]),
        mesh=mesh,
        in_specs=(
            P("section", "dp", None),
            P("section", "dp", None, None),
            P("section", "dp", None, None),
            P("section", None, None, "dp"),
            P(None, None, "dp"),
            P(),
            P("dp"),
        ),
        out_specs=(
            P("section", None, None, "dp"),
            P("section", "dp", None, None),
            P("section", "dp", None, None),
        ),
        check_vma=False,
    )
```

time: 321 us -> 94.3 us (0.29)
  blocking collectives: 166 us -> 0 us
  matrix products: 103 us -> 0 us
  Pallas kernels: 0 us -> 79.3 us
  starting transfers between devices: 20.3 us -> 0 us
  other arithmetic: 22.2 us -> 2.9 us
  local copies, waits for them, and re-layouts: 1.14 us -> 10.8 us
  waiting for transfers between devices: 3.35 us -> 0 us
    all_gather x8 -> x0, blocking collectives: 124 us -> none  [the longest x4 64.4 us: step(): lax.all_gather(inputs_cols, 'dp', axis=1, tiled=True)]
    dot_general x40 -> x0, matrix products: 103 us -> none  [the longest x4 40.9 us: step(): lax.dot_general(grad_full, w_rows, (((1,), (1,)), ((), ())), preferred_el...]
    pallas_call x0 -> x2, Pallas kernels: none -> 79.3 us  [the longest x1 72.7 us: per_device(): pl.pallas_call(functools.partial(chain_kernel, n_sec, n_dp, rank, pack, l...]
    psum x1 -> x0, blocking collectives: 42.4 us -> none  [per_device(): total = lax.psum(local_sq, ('section', 'dp'))]
    all_to_all x4 -> x0, starting transfers between devices: 15.2 us -> none  [step(): lax.all_to_all(terms, 'dp', split_axis=1, concat_axis=0, tiled=True)]
    unnamed x8 -> x18, local copies, waits for them, and re-layouts: 0.02 us -> 8.14 us
    reduce_sum x6 -> x2, other arithmetic: 6.27 us -> 0.17 us  [the longest x1 0.09 us: per_device(): w2 = jnp.sum(jnp.where(held, (weights * weights)[None, :], 0.0), axis=1)]
    broadcast_in_dim x2 -> x0, other arithmetic: 5.98 us -> none  [the longest x1 4.16 us: per_device(): (scaled_up * factor).astype(jnp.bfloat16)[None]]
  transfers between devices with their start and end apart: 8 -> 0, of which waited for: 4 -> 0; matrix products, arithmetic and copies ran while one was open for 26% -> 0% of each run, Pallas kernels for 0% -> 0%
where the time goes in v1:
time: 94.3 us; the launch traced here: 93.6 us
  Pallas kernels  79.3 us (84%)
  local copies, waits for them, and re-layouts  10.8 us (11%)
  other arithmetic  2.9 us (3%)
    pallas_call x1, Pallas kernels, per_device(): pl.pallas_call(functools.partial(chain_kernel, n_sec, n_dp, rank, pack, l...  72.7 us
    unnamed x18, local copies, waits for them, and re-layouts  8.14 us
    pallas_call x1, Pallas kernels, per_device(): pl.pallas_call(write_kernel, grid=(n_dp,), out_shape=(jax.ShapeDtypeStruc...  6.58 us

profile of v1, /device:TPU:0, one launch (start us, length us, event | category | flops | bytes accessed | tf_op | source)
XLA Modules:
  0.0 93.6 jit_solution(4537020720176461565)
XLA Ops:
  0.6 0.7 and_select_fusion.1
  1.3 0.7 fusion.2
  2.0 0.1 convert_reduce_fusion
  2.1 0.7 multiply_add_fusion
  2.7 0.7 fusion.3
  3.4 0.1 broadcast_in_dim.53
  3.5 0.1 iota_add_fusion
  3.5 0.1 add.52
  3.6 0.7 broadcast_in_dim.45
  4.4 0.1 reshape.69
  4.4 0.1 fusion.1
  4.5 0.1 copy.20.w2_col
  4.6 0.1 copy.18.sens_col
  4.7 0.1 copy.19.tgt_col
  4.8 0.8 broadcast_in_dim_reshape.8.scale_ref
  5.6 0.0 copy-start
  5.6 1.6 %copy-done = bf16[1,2,8192,64]{2,3,1,0:T(8,128)(2,1)S(1)} copy-done((bf16[1,2,8192,64]{2,3,1,0:T(8,128)(2,1)S(1)}, bf16[1,2,8192,64]{2,3,1,0:T(8,128)(2,1)}, u32[]{:S(2)}) %copy-start) | copy-done | bytes 2097176
  7.2 0.0 copy-start.1
  7.2 1.6 %copy-done.1 = bf16[1,2,64,8192]{3,2,1,0:T(8,128)(2,1)S(1)} copy-done((bf16[1,2,64,8192]{3,2,1,0:T(8,128)(2,1)S(1)}, bf16[1,2,64,8192]{3,2,1,0:T(8,128)(2,1)}, u32[]{:S(2)}) %copy-start.1) | copy-done | bytes 2097176
  8.7 0.0 copy-start.4
  8.7 0.8 copy-done.4
  9.5 0.0 copy-start.5
  9.5 0.8 copy-done.5
  10.3 72.7 %chain.1 = (bf16[32,1024]{1,0:T(8,128)(2,1)S(1)}, bf16[8,32,1024]{2,1,0:T(8,128)(2,1)S(1)}, bf16[8,32,1024]{2,1,0:T(8,128)(2,1)S(1)}, bf16[32,128]{1,0:T(8,128)(...) custom-call(bf16[1024,8192]{1,0:T(8,128)(2,1)} %bitcast.34, bf16[128,8192]{1,0:T(8,128)(2,1)S(1)} %bitcast.30, ...), custom_call_target="tpu_custom_call" | custom-call | tf_op jit(solution)/shard_map/chain/pallas_call | solution.py:375
  83.1 0.0 copy-start.2
  83.1 0.8 copy-done.2
  83.9 0.0 copy-start.3
  83.9 0.8 copy-done.3
  84.7 0.0 copy-start.6
  84.7 0.6 copy-done.6
  85.3 0.0 copy-start.7
  85.3 0.6 copy-done.7
  85.8 0.0 copy-start.8
  85.8 0.6 copy-done.8
  86.4 0.6 slice_bitcast_fusion
  87.1 6.6 %write.1 = (bf16[128,8192]{1,0:T(8,128)(2,1)}, bf16[128,8192]{1,0:T(8,128)(2,1)}) custom-call(bf16[8,32,1024]{2,1,0:T(8,128)(2,1)} %copy-done.2, bf16[8,32,1024]{2,1,0:T(8,128)(2,1)} %copy-done.3, bf16[32,128]{1,0:T(8,128)(2,1)} %copy-done.6, bf16[32,128]{1,0:T(8,128)(2,1)} %copy-done.7, f32[1,128]{1,0:T(1,128)} %copy-done.8, ...), custom_call_target="tpu_custom_call" | custom-call | tf_op jit(solution)/shard_map/write/pallas_call | solution.py:438
  (3 shorter events, 0.0 us)
Async XLA Ops:
  5.6 1.6 %copy-start = (bf16[1,2,8192,64]{2,3,1,0:T(8,128)(2,1)S(1)}, bf16[1,2,8192,64]{2,3,1,0:T(8,128)(2,1)}, u32[]{:S(2)}) copy-start(bf16[1,2,8192,64]{2,3,1,0:T(8,128)(2,1)} %param.8) | copy-start | bytes 6291460
  7.2 1.6 %copy-start.1 = (bf16[1,2,64,8192]{3,2,1,0:T(8,128)(2,1)S(1)}, bf16[1,2,64,8192]{3,2,1,0:T(8,128)(2,1)}, u32[]{:S(2)}) copy-start(bf16[1,2,64,8192]{3,2,1,0:T(8,128)(2,1)} %param.9) | copy-start | bytes 6291460
  8.7 0.8 copy-start.4
  9.5 0.8 copy-start.5
  83.1 0.8 copy-start.2
  83.9 0.8 copy-start.3
  84.7 0.6 copy-start.6
  85.3 0.6 copy-start.7
  85.8 0.6 copy-start.8

commit v2 on v1

--- a/solution.py
+++ b/solution.py
@@ -25,10 +25,11 @@
 
 
 def chain_kernel(
-    n_sec, n_dp, rank, pack, limit,
-    w_hbm, dn_hbm, up_hbm, x_in, g_in, sens_col, tgt_col, tgt_row, w2_col,
-    res_out, x_out, g_out, u_out, v_out, fac_out,
-    wbuf, dbuf, ubuf, xbuf, gbuf, lsend, lrecv, acc, uacc, vacc, gram_x, chain_in, chain_out, norms,
+    n_sec, n_dp, rank, pack, fold, limit,
+    sensor, counts, w_hbm, dn_hbm, up_hbm, x_in, g_in,
+    res_out, down_hbm, up_grad_hbm, fac_out,
+    wbuf, dbuf, ubuf, xbuf, gbuf, rbuf, u_out, v_out, dprod, uprod,
+    lsend, lrecv, acc, uacc, vacc, gram_x, chain_in, chain_out, norms,
     w_sem, a_sem, o_sem, x_rs, x_ss, x_fs, g_rs, og_ss, g_ss, g_fs, l_ss, l_rs, c_ss, c_rs, n_ss, n_rs,
 ):
     sec = lax.axis_index("section")
@@ -41,7 +42,9 @@
     top = n_sec - 1
     is_top = sec == top
     tokens, columns = x_in.shape
-    rows = xbuf.shape[1]
+    rows = tokens
+    block_rows = tokens // n_dp
+    sen_local = uacc.shape[1] // rank
     wide = columns // pack
     lanes = uacc.shape[1]
 
@@ -79,18 +82,53 @@
             return carry
         lax.fori_loop(0, n_dp, greet, 0)
 
-    def padded(ref):
-        value = ref[...]
-        if rows == tokens:
+    def folded(value):
+        if fold == 1:
+            return value.astype(jnp.bfloat16)
+        side = columns // 2
+        return jnp.concatenate([value[:, :side], value[:, side:]], axis=0).astype(jnp.bfloat16)
+
+    def unfolded(value):
+        if fold == 1:
             return value
-        tail = jnp.zeros((rows - tokens, columns), jnp.float32)
-        return jnp.concatenate([value.astype(jnp.float32), tail], axis=0).astype(jnp.bfloat16)
-
-    xbuf[me] = padded(x_in)
+        value = value.astype(jnp.float32)
+        return jnp.concatenate([value[:rows], value[rows:]], axis=1).astype(jnp.bfloat16)
+
+    xbuf[me] = folded(x_in[...].astype(jnp.float32))
 
     @pl.when(is_top)
     def _():
-        gbuf[me] = padded(g_in)
+        gbuf[me] = folded(g_in[...].astype(jnp.float32))
+
+    col_block = lax.broadcasted_iota(jnp.int32, (rows, 1), 0) // block_rows
+    row_block = lax.broadcasted_iota(jnp.int32, (1, rows), 1) // block_rows
+
+    def fill(b, carry):
+        col, row = carry
+        ident = sensor[0, b]
+        return jnp.where(col_block == b, ident, col), jnp.where(row_block == b, ident, row)
+
+    sens_col, sens_row = lax.fori_loop(
+        0, n_dp, fill, (jnp.zeros((rows, 1), jnp.int32), jnp.zeros((1, rows), jnp.int32))
+    )
+    own_col, own_row = sens_col // sen_local, sens_row // sen_local
+    col_at = lax.broadcasted_iota(jnp.int32, (rows, rows), 0)
+    row_at = lax.broadcasted_iota(jnp.int32, (rows, rows), 1)
+    same = own_col == own_row
+    head_col = same & (col_at // block_rows < row_block) & (lax.rem(col_at, block_rows) == 0)
+    head_row = same & (row_at // block_rows < col_block) & (lax.rem(row_at, block_rows) == 0)
+    pos_row = jnp.sum(jnp.where(head_col, 1.0, 0.0), axis=0, keepdims=True)
+    pos_col = jnp.sum(jnp.where(head_row, 1.0, 0.0), axis=1, keepdims=True)
+    in_row = lax.rem(lax.broadcasted_iota(jnp.int32, (1, rows), 1), block_rows)
+    in_col = lax.rem(lax.broadcasted_iota(jnp.int32, (rows, 1), 0), block_rows)
+    tgt_row = own_row * SLOT + pos_row.astype(jnp.int32) * block_rows + in_row
+    tgt_col = own_col * SLOT + pos_col.astype(jnp.int32) * block_rows + in_col
+    w2_col = jnp.zeros((rows, 1), jnp.float32)
+    for i in range(sen_local):
+        weight = SCALE * NORM_TOK / jnp.full((rows, 1), counts[i], jnp.int32).astype(jnp.float32)
+        w2_col = jnp.where(sens_col == me * sen_local + i, weight * weight, w2_col)
+    lane_sensor = lax.broadcasted_iota(jnp.int32, (rows, lanes), 1) // rank
+    own = sens_col == me * sen_local + lane_sensor
 
     pl.semaphore_wait(barrier, n_sec * n_dp - 1)
 
@@ -112,7 +150,7 @@
         return remote(gbuf.at[j], gbuf.at[j], g_fs.at[j // 2], g_rs.at[j], sec, partner)
 
     def res_copy(k):
-        return remote(res_out, gbuf.at[me], g_ss.at[k], g_rs.at[me], sec - 1, 2 * near(k) + par)
+        return remote(rbuf, gbuf.at[me], g_ss.at[k], g_rs.at[me], sec - 1, 2 * near(k) + par)
 
     def low_copy(j):
         return remote(lsend.at[j], lrecv.at[me], l_ss.at[j], l_rs.at[me], sec, j)
@@ -126,16 +164,13 @@
             return carry
         lax.fori_loop(lo, hi, step, 0)
 
-    lane_sensor = lax.broadcasted_iota(jnp.int32, (rows, lanes), 1) // rank
-    own = sens_col[...] == me * (lanes // rank) + lane_sensor
-
     def x_work():
         loop(1, half, lambda k: x_copy(k).start())
         vacc[...] = jnp.zeros_like(vacc)
         gram_x[...] = jnp.zeros_like(gram_x)
 
         def use(j):
-            piece = xbuf[j]
+            piece = unfolded(xbuf[j])
             vacc[...] += mm_t(piece, dbuf[:, cols(j)])
             gram_x[...] += mm_t(piece, piece)
 
@@ -156,7 +191,6 @@
         loop(0, half, first)
         loop(0, half, second)
         v_out[...] = jnp.where(own, vacc[...], 0.0).astype(jnp.bfloat16)
-        pltpu.make_async_copy(xbuf, x_out, o_sem.at[0]).start()
 
     @pl.when(is_top)
     def _():
@@ -180,14 +214,14 @@
             g_forward(j).wait_recv()
         g_forward(j).start()
         w_copy(j).wait()
-        piece = gbuf[j]
+        piece = unfolded(gbuf[j])
         uacc[...] += mm_t(piece, ubuf[:, cols(j)])
         acc[...] += mm_t(piece, wbuf[:, cols(j)])
 
     def g_second(k):
         j = 2 * near(k) + 1 - par
         g_forward(j).wait_recv()
-        uacc[...] += mm_t(gbuf[j], ubuf[:, cols(j)])
+        uacc[...] += mm_t(unfolded(gbuf[j]), ubuf[:, cols(j)])
 
     loop(0, half, g_first)
     loop(0, half, g_second)
@@ -195,7 +229,7 @@
 
     slot_at = lax.broadcasted_iota(jnp.int32, (SLOT, rows), 0) + me * SLOT
     in_slot = lax.broadcasted_iota(jnp.int32, (SLOT, rows), 0) < SLOT // pack
-    select = jnp.where((tgt_row[...] == slot_at) & in_slot, 1.0, 0.0).astype(jnp.bfloat16)
+    select = jnp.where((tgt_row == slot_at) & in_slot, 1.0, 0.0).astype(jnp.bfloat16)
     u_sel = mm(select, u_out[...]).astype(jnp.bfloat16)
 
     def low_work(k):
@@ -224,12 +258,12 @@
 
     def norm_value():
         def add(j, total):
-            piece = gbuf[j]
+            piece = unfolded(gbuf[j])
             return total + mm_t(piece, piece)
         gram_g = lax.fori_loop(0, n_dp, add, jnp.zeros((rows, rows), jnp.float32))
         uu = mm_t(u_out[...], u_out[...])
         vv = mm_t(v_out[...], v_out[...])
-        whole = jnp.sum((gram_x[...] * uu + gram_g * vv) * w2_col[...], axis=0, keepdims=True)
+        whole = jnp.sum((gram_x[...] * uu + gram_g * vv) * w2_col, axis=0, keepdims=True)
         return jnp.broadcast_to(jnp.sum(whole, axis=1, keepdims=True), (1, 128))
 
     @pl.when(sec == 0)
@@ -247,7 +281,7 @@
     def g_third(k):
         j = 2 * near(k) + 1 - par
         w_copy(j).wait()
-        acc[...] += mm_t(gbuf[j], wbuf[:, cols(j)])
+        acc[...] += mm_t(unfolded(gbuf[j]), wbuf[:, cols(j)])
 
     loop(0, half, g_third)
 
@@ -261,15 +295,16 @@
     lane_at = lax.broadcasted_iota(jnp.int32, (rows, n_dp * SLOT), 1)
     parts = []
     for h in range(pack):
-        place = jnp.where(tgt_col[...] + h * (SLOT // 2) == lane_at, 1.0, 0.0).astype(jnp.bfloat16)
+        place = jnp.where(tgt_col + h * (SLOT // 2) == lane_at, 1.0, 0.0).astype(jnp.bfloat16)
         parts.append(acc[:, h * wide : (h + 1) * wide] + mm(place, terms))
-    res_out[...] = (parts[0] if pack == 1 else jnp.concatenate(parts, axis=1)).astype(jnp.bfloat16)
+    result = parts[0] if pack == 1 else jnp.concatenate(parts, axis=1)
+    rbuf[...] = folded(result)
 
     @pl.when(sec > 0)
     def _():
         loop(0, half, lambda k: res_copy(k).start())
 
-    pltpu.make_async_copy(gbuf, g_out, o_sem.at[1]).start()
+    res_out[...] = result.astype(jnp.bfloat16)
 
     @pl.when(is_top)
     def _():
@@ -289,6 +324,23 @@
             chain_out[...] = value + chain_in[...]
         chain_copy().start()
 
+    def down_copy(j):
+        return pltpu.make_async_copy(dprod.at[:, cols(j)], down_hbm.at[:, cols(j)], o_sem.at[0, j])
+
+    def up_grad_copy(j):
+        return pltpu.make_async_copy(uprod.at[:, cols(j)], up_grad_hbm.at[:, cols(j)], o_sem.at[1, j])
+
+    u_t = u_out[...].astype(jnp.float32).T.astype(jnp.bfloat16)
+    v_t = v_out[...].astype(jnp.float32).T.astype(jnp.bfloat16)
+
+    def grow(j):
+        dprod[:, cols(j)] = mm(u_t, unfolded(xbuf[j])).astype(jnp.bfloat16)
+        down_copy(j).start()
+        uprod[:, cols(j)] = mm(v_t, unfolded(gbuf[j])).astype(jnp.bfloat16)
+        up_grad_copy(j).start()
+
+    loop(0, n_dp, grow)
+
     def norm_wait(j):
         @pl.when((sec != 0) | (me != j))
         def _():
@@ -313,8 +365,8 @@
             low_copy(j).wait_send()
 
     loop(0, n_dp, low_sent)
-    pltpu.make_async_copy(xbuf, x_out, o_sem.at[0]).wait()
-    pltpu.make_async_copy(gbuf, g_out, o_sem.at[1]).wait()
+    loop(0, n_dp, lambda j: down_copy(j).wait())
+    loop(0, n_dp, lambda j: up_grad_copy(j).wait())
 
     loop(0, n_dp, norm_wait)
     total = jnp.maximum(jnp.sum(norms[...], axis=0), 0.0)
@@ -330,41 +382,15 @@
             loop(0, n_dp, sent)
 
 
-def write_kernel(x_ref, g_ref, u_ref, v_ref, fac_ref, scale_ref, down_ref, up_ref):
-    scale = scale_ref[...] * fac_ref[0:1, 0:1]
-    tn = (((0,), (0,)), ((), ()))
-    down = lax.dot_general(u_ref[...], x_ref[0], tn, preferred_element_type=jnp.float32)
-    down_ref[...] = (down * scale).astype(jnp.bfloat16)
-    up = lax.dot_general(v_ref[...], g_ref[0], tn, preferred_element_type=jnp.float32)
-    up_ref[...] = (up * scale).astype(jnp.bfloat16)
-
-
 def per_device(n_sec, n_dp, frozen, adapt_down, adapt_up, saved_inputs, out_grad, sensor, counts):
-    me = lax.axis_index("dp")
     tokens, columns = out_grad.shape[1:]
     width = columns * n_dp
-    blocks = sensor.shape[1]
-    block_rows = tokens // blocks
     sen_local, rank = adapt_up.shape[1:3]
     lanes = sen_local * rank
-    rows = -(-tokens // 16) * 16
     pack = 2 if columns % 256 == 0 else 1
+    fold = 2 if tokens % 16 else 1
+    rows = tokens
     w_rows = frozen.shape[1]
-
-    idents = sensor[0]
-    owners = idents // sen_local
-    order = jnp.arange(blocks, dtype=jnp.int32)
-    earlier = (owners[:, None] == owners[None, :]) & (order[:, None] < order[None, :])
-    position = jnp.sum(earlier.astype(jnp.int32), axis=0)
-    first = owners * SLOT + position * block_rows
-    target = (first[:, None] + jnp.arange(block_rows, dtype=jnp.int32)[None, :]).reshape(-1)
-    more = (0, rows - tokens)
-    target = jnp.pad(target, more, constant_values=-SLOT)
-    sens = jnp.pad(jnp.repeat(idents, block_rows), more, constant_values=-1)
-    weights = SCALE * (NORM_TOK / counts.astype(jnp.float32))
-    held = sens[:, None] == me * sen_local + jnp.arange(sen_local, dtype=jnp.int32)[None, :]
-    w2 = jnp.sum(jnp.where(held, (weights * weights)[None, :], 0.0), axis=1)
-    scale_col = jnp.repeat(weights, rank)[:, None]
     limit = CLIP_RMS * math.sqrt(2.0 * n_sec * n_dp * sen_local * width * rank)
 
     bf, f32 = jnp.bfloat16, jnp.float32
@@ -372,24 +398,28 @@
     anywhere = pl.BlockSpec(memory_space=pl.ANY)
     half = n_dp // 2
     dma = pltpu.SemaphoreType.DMA
-    result, x_full, g_full, u, v, factor = pl.pallas_call(
-        functools.partial(chain_kernel, n_sec, n_dp, rank, pack, limit),
+    smem = pl.BlockSpec(memory_space=pltpu.SMEM)
+    result, down, up, factor = pl.pallas_call(
+        functools.partial(chain_kernel, n_sec, n_dp, rank, pack, fold, limit),
         out_shape=(
             jax.ShapeDtypeStruct((rows, columns), bf),
-            jax.ShapeDtypeStruct((n_dp, rows, columns), bf),
-            jax.ShapeDtypeStruct((n_dp, rows, columns), bf),
-            jax.ShapeDtypeStruct((rows, lanes), bf),
-            jax.ShapeDtypeStruct((rows, lanes), bf),
+            jax.ShapeDtypeStruct((lanes, width), bf),
+            jax.ShapeDtypeStruct((lanes, width), bf),
             jax.ShapeDtypeStruct((1, 128), f32),
         ),
-        in_specs=[anywhere] * 3 + [vm] * 6,
-        out_specs=(vm, anywhere, anywhere, vm, vm, vm),
+        in_specs=[smem] * 2 + [anywhere] * 3 + [vm] * 2,
+        out_specs=(vm, anywhere, anywhere, vm),
         scratch_shapes=[
             pltpu.VMEM((w_rows, width), bf),
             pltpu.VMEM((lanes, width), bf),
             pltpu.VMEM((lanes, width), bf),
-            pltpu.VMEM((n_dp, rows, columns), bf),
-            pltpu.VMEM((n_dp, rows, columns), bf),
+            pltpu.VMEM((n_dp, rows * fold, columns // fold), bf),
+            pltpu.VMEM((n_dp, rows * fold, columns // fold), bf),
+            pltpu.VMEM((rows * fold, columns // fold), bf),
+            pltpu.VMEM((rows, lanes), bf),
+            pltpu.VMEM((rows, lanes), bf),
+            pltpu.VMEM((lanes, width), bf),
+            pltpu.VMEM((lanes, width), bf),
             pltpu.VMEM((n_dp, SLOT, columns // pack), bf),
             pltpu.VMEM((n_dp, SLOT, columns // pack), bf),
             pltpu.VMEM((rows, columns), f32),
@@ -401,7 +431,7 @@
             pltpu.VMEM((n_dp, 1, 128), f32),
             dma((n_dp,)),
             dma((2,)),
-            dma((2,)),
+            dma((2, n_dp)),
             dma((n_dp,)),
             dma((half,)),
             dma((half,)),
@@ -417,37 +447,22 @@
             dma((n_dp,)),
         ],
         compiler_params=pltpu.CompilerParams(
-            collective_id=0, has_side_effects=True, vmem_limit_bytes=48 * 1024 * 1024
+            collective_id=0, has_side_effects=True, vmem_limit_bytes=60 * 1024 * 1024
         ),
         name="chain",
     )(
+        sensor,
+        counts,
         frozen[0],
         jnp.swapaxes(adapt_down[0], 1, 2).reshape(lanes, width),
         adapt_up[0].reshape(lanes, width),
         saved_inputs[0, 0],
         out_grad[0],
-        sens[:, None],
-        target[:, None],
-        target[None, :],
-        w2[:, None],
     )
-
-    fixed = lambda shape: pl.BlockSpec(shape, lambda j: (0, 0))
-    piece = pl.BlockSpec((1, rows, columns), lambda j: (j, 0, 0))
-    grown = pl.BlockSpec((lanes, columns), lambda j: (0, j))
-    down, up = pl.pallas_call(
-        write_kernel,
-        grid=(n_dp,),
-        out_shape=(jax.ShapeDtypeStruct((lanes, width), bf),) * 2,
-        in_specs=[piece, piece, fixed((rows, lanes)), fixed((rows, lanes)), fixed((1, 128)), fixed((lanes, 1))],
-        out_specs=(grown, grown),
-        name="write",
-    )(x_full, g_full, u, v, factor, scale_col)
-    return (
-        result[:tokens][None, None],
-        jnp.swapaxes(down.reshape(sen_local, rank, width), 1, 2)[None],
-        up.reshape(sen_local, rank, width)[None],
-    )
+    scale = (SCALE * NORM_TOK / counts.astype(f32) * factor[0, 0])[:, None, None]
+    down = (down.reshape(sen_local, rank, width) * scale).astype(bf)
+    up = (up.reshape(sen_local, rank, width) * scale).astype(bf)
+    return result[None, None], jnp.swapaxes(down, 1, 2)[None], up[None]
 
 
 def solution(mesh):

time: 94.3 us -> 77.6 us (0.82)
  local copies, waits for them, and re-layouts: 10.8 us -> 0.63 us
  Pallas kernels: 79.3 us -> 70.2 us
  other arithmetic: 2.9 us -> 5.9 us
    pallas_call x2 -> x1, Pallas kernels: 79.3 us -> 70.2 us  [per_device(): pl.pallas_call(functools.partial(chain_kernel, n_sec, n_dp, rank, pack, f...]
    unnamed x18 -> x7, local copies, waits for them, and re-layouts: 8.14 us -> 0.63 us
    convert_element_type x0 -> x1, other arithmetic: none -> 3.51 us  [per_device(): up = (up.reshape(sen_local, rank, width) * scale).astype(bf)]
    broadcast_in_dim x0 -> x1, other arithmetic: none -> 1.77 us  [per_device(): return (result[None, None], jnp.swapaxes(down, 1, 2)[None], up[None])]
    broadcast_in_dim x7 -> x0, local copies, waits for them, and re-layouts: 1.69 us -> none  [the longest x1 0.73 us: per_device(): sens = jnp.pad(jnp.repeat(idents, block_rows), more, constant_values=-1)]
where the time goes in v2:
time: 77.6 us; the launch traced here: 77.4 us
  Pallas kernels  70.2 us (90%)
  other arithmetic  5.9 us (8%)
    pallas_call x1, Pallas kernels, per_device(): pl.pallas_call(functools.partial(chain_kernel, n_sec, n_dp, rank, pack, f...  70.2 us
    convert_element_type x1, other arithmetic, per_device(): up = (up.reshape(sen_local, rank, width) * scale).astype(bf)  3.51 us
    broadcast_in_dim x1, other arithmetic, per_device(): return (result[None, None], jnp.swapaxes(down, 1, 2)[None], up[None])  1.77 us

profile of v2, /device:TPU:0, one launch (start us, length us, event | category | flops | bytes accessed | tf_op | source)
XLA Modules:
  0.0 77.4 jit_solution(13140430348487078468)
XLA Ops:
  0.6 0.0 copy-start.2
  0.6 70.2 %chain.1 = (bf16[24,1024]{1,0:T(8,128)(2,1)}, bf16[128,8192]{1,0:T(8,128)(2,1)}, bf16[128,8192]{1,0:T(8,128)(2,1)}, f32[1,128]{1,0:T(1,128)}) custom-call(s32[1,8]{1,0:T(1,128)} %sensor.1, s32[2]{0:T(128)} %counts.1, bf16[1024,8192]{1,0:T(8,128)(2,1)} %bitcast.20, bf16[128,8192]{1,0:T(8,128)(2,1)} %bitcast.23, bf16[128,8192]{1,0:T(8,128)(2,1)} %bitcast.24, ...), custom_call_target="tpu_custom_call" | custom-call | tf_op jit(solution)/shard_map/chain/pallas_call | solution.py:402
  70.9 0.0 copy-done.2
  70.9 0.6 divide_multiply_fusion
  71.5 0.0 copy-start
  71.5 3.5 %fusion = bf16[1,2,64,8192]{3,2,1,0:T(8,128)(2,1)} fusion(bf16[1,2,64,8192]{3,2,1,0:T(8,128)(2,1)} %bitcast.22, f32[2]{0:T(128)S(1)} %divide_multiply_fusion), kind=kLoop, calls=%fused_computation.1 | loop fusion | flops 3145728 | bytes 4194312 | tf_op jit(solution)/shard_map/convert_element_type | solution.py:464
  75.0 0.0 copy-done
  75.0 0.0 copy-start.1
  75.0 1.8 %fusion.2 = bf16[1,2,8192,64]{2,3,1,0:T(8,128)(2,1)} fusion(bf16[2,64,8192]{2,1,0:T(8,128)(2,1)S(1)} %bitcast.21, f32[2]{0:T(128)S(1)} %divide_multiply_fusion), kind=kLoop, calls=%fused_computation.4 | loop fusion | flops 3145728 | bytes 4194312 | tf_op jit(solution)/shard_map/broadcast_in_dim | solution.py:465
  76.8 0.0 copy-done.1
  76.8 0.6 copy.11
Async XLA Ops:
  0.6 70.2 %copy-start.2 = (s32[2]{0:T(128)S(1)}, s32[2]{0:T(128)}, u32[]{:S(2)}) copy-start(s32[2]{0:T(128)} %counts.1) | copy-start | bytes 28
  71.5 3.5 %copy-start = (bf16[128,8192]{1,0:T(8,128)(2,1)S(1)}, bf16[128,8192]{1,0:T(8,128)(2,1)}, u32[]{:S(2)}) copy-start(bf16[128,8192]{1,0:T(8,128)(2,1)} %get-tuple-element.8) | copy-start | bytes 6291460
  75.0 1.8 %copy-start.1 = (bf16[24,1024]{1,0:T(8,128)(2,1)S(1)}, bf16[24,1024]{1,0:T(8,128)(2,1)}, u32[]{:S(2)}) copy-start(bf16[24,1024]{1,0:T(8,128)(2,1)} %get-tuple-element.7) | copy-start | bytes 147460

commit v3 on v2

--- a/solution.py
+++ b/solution.py
@@ -29,8 +29,8 @@
     sensor, counts, w_hbm, dn_hbm, up_hbm, x_in, g_in,
     res_out, down_hbm, up_grad_hbm, fac_out,
     wbuf, dbuf, ubuf, xbuf, gbuf, rbuf, u_out, v_out, dprod, uprod,
-    lsend, lrecv, acc, uacc, vacc, gram_x, chain_in, chain_out, norms,
-    w_sem, a_sem, o_sem, x_rs, x_ss, x_fs, g_rs, og_ss, g_ss, g_fs, l_ss, l_rs, c_ss, c_rs, n_ss, n_rs,
+    lsend, lrecv, acc, uacc, vacc, gram_x, chain_in, chain_out, norms, total_in,
+    w_sem, a_sem, o_sem, x_rs, x_ss, x_fs, g_rs, og_ss, g_ss, g_fs, l_ss, l_rs, c_ss, c_rs, n_ss, n_rs, t_ss, t_rs,
 ):
     sec = lax.axis_index("section")
     me = lax.axis_index("dp")
@@ -74,13 +74,42 @@
     lax.fori_loop(0, half, start_w_other, 0)
 
     barrier = pltpu.get_barrier_semaphore()
-    for q in range(n_sec):
-        def greet(d, carry, q=q):
-            @pl.when((sec != q) | (me != d))
-            def _():
-                pl.semaphore_signal(barrier, inc=1, device_id=(q, d), device_id_type=MESH)
-            return carry
-        lax.fori_loop(0, n_dp, greet, 0)
+    def greet(q, d):
+        pl.semaphore_signal(barrier, inc=1, device_id=(q, d), device_id_type=MESH)
+
+    def greet_own(k, carry):
+        greet(sec, lax.rem(me + k, n_dp))
+        return carry
+
+    def greet_below(k, carry):
+        greet(sec - 1, 2 * near(k) + par)
+        return carry
+
+    def greet_above(k, carry):
+        greet(sec + 1, 2 * near(k) + par)
+        return carry
+
+    lax.fori_loop(1, n_dp, greet_own, 0)
+
+    @pl.when(sec > 0)
+    def _():
+        lax.fori_loop(0, half, greet_below, 0)
+
+    @pl.when(sec < top)
+    def _():
+        lax.fori_loop(0, half, greet_above, 0)
+
+    @pl.when(sec == 0)
+    def _():
+        for q in range(2, n_sec):
+            greet(q, me)
+
+    @pl.when(sec > 1)
+    def _():
+        greet(0, me)
+
+    greeted = n_dp - 1 + jnp.where(sec > 0, half, 0) + jnp.where(sec < top, half, 0)
+    greeted = greeted + jnp.where(sec == 0, n_sec - 2, jnp.where(sec > 1, 1, 0))
 
     def folded(value):
         if fold == 1:
@@ -130,7 +159,7 @@
     lane_sensor = lax.broadcasted_iota(jnp.int32, (rows, lanes), 1) // rank
     own = sens_col == me * sen_local + lane_sensor
 
-    pl.semaphore_wait(barrier, n_sec * n_dp - 1)
+    pl.semaphore_wait(barrier, greeted)
 
     def remote(src, dst, ss, rs, q, d):
         return pltpu.make_async_remote_copy(
@@ -163,6 +192,13 @@
             body(k)
             return carry
         lax.fori_loop(lo, hi, step, 0)
+
+    def loop_flat(lo, hi, body):
+        if hi - lo > 8:
+            loop(lo, hi, body)
+        else:
+            for k in range(lo, hi):
+                body(k)
 
     def x_work():
         loop(1, half, lambda k: x_copy(k).start())
@@ -224,7 +260,7 @@
         uacc[...] += mm_t(unfolded(gbuf[j]), ubuf[:, cols(j)])
 
     loop(0, half, g_first)
-    loop(0, half, g_second)
+    loop_flat(0, half, g_second)
     u_out[...] = jnp.where(own, uacc[...], 0.0).astype(jnp.bfloat16)
 
     slot_at = lax.broadcasted_iota(jnp.int32, (SLOT, rows), 0) + me * SLOT
@@ -232,29 +268,28 @@
     select = jnp.where((tgt_row == slot_at) & in_slot, 1.0, 0.0).astype(jnp.bfloat16)
     u_sel = mm(select, u_out[...]).astype(jnp.bfloat16)
 
-    def low_work(k):
-        j = lax.rem(me + k, n_dp)
+    def low_of(j):
         low = SCALE * mm(u_sel, dbuf[:, cols(j)])
         if pack == 2:
             low = jnp.concatenate([low[: SLOT // 2, :wide], low[: SLOT // 2, wide:]], axis=0)
-        low = low.astype(jnp.bfloat16)
-
-        @pl.when(k < n_dp)
-        def _():
-            lsend[j] = low
-            low_copy(j).start()
-
-        @pl.when(k == n_dp)
-        def _():
-            lrecv[me] = low
-
-    loop(1, n_dp + 1, low_work)
+        return low.astype(jnp.bfloat16)
+
+    def low_work(k):
+        j = lax.rem(me + k, n_dp)
+        lsend[j] = low_of(j)
+        low_copy(j).start()
+
+    loop_flat(1, n_dp, low_work)
+    lrecv[me] = low_of(me)
 
     def chain_copy():
         return remote(chain_out, chain_in, c_ss, c_rs, sec - 1, me)
 
-    def norm_copy(q, d):
-        return remote(norms.at[me], norms.at[me], n_ss.at[q, d], n_rs.at[me], q, d)
+    def norm_copy(d):
+        return remote(norms.at[me], norms.at[me], n_ss.at[d], n_rs.at[me], 0, d)
+
+    def total_copy(q):
+        return remote(total_in, total_in, t_ss.at[q], t_rs, q, me)
 
     def norm_value():
         def add(j, total):
@@ -271,19 +306,25 @@
         value = norm_value()
         chain_copy().wait_recv()
         norms[me] = value + chain_in[...]
-        for q in range(n_sec):
-            def send(d, q=q):
-                @pl.when((me != d) | (q != 0))
-                def _():
-                    norm_copy(q, d).start()
-            loop(0, n_dp, send)
+        loop(1, n_dp, lambda k: norm_copy(lax.rem(me + k, n_dp)).start())
 
     def g_third(k):
         j = 2 * near(k) + 1 - par
         w_copy(j).wait()
         acc[...] += mm_t(unfolded(gbuf[j]), wbuf[:, cols(j)])
 
-    loop(0, half, g_third)
+    loop_flat(0, half, g_third)
+
+    def norm_wait(k):
+        j = lax.rem(me + k, n_dp)
+        remote(norms.at[j], norms.at[j], n_ss.at[j], n_rs.at[j], 0, partner).wait_recv()
+
+    @pl.when(sec == 0)
+    def _():
+        loop(1, n_dp, norm_wait)
+        total_in[...] = jnp.sum(norms[...], axis=0)
+        for q in range(1, n_sec):
+            total_copy(q).start()
 
     def low_wait(j):
         @pl.when(j != me)
@@ -341,11 +382,6 @@
 
     loop(0, n_dp, grow)
 
-    def norm_wait(j):
-        @pl.when((sec != 0) | (me != j))
-        def _():
-            remote(norms.at[j], norms.at[j], n_ss.at[0, j], n_rs.at[j], 0, partner).wait_recv()
-
     @pl.when(is_top)
     def _():
         loop(1, half, lambda k: og_copy(k).wait_send())
@@ -368,18 +404,18 @@
     loop(0, n_dp, lambda j: down_copy(j).wait())
     loop(0, n_dp, lambda j: up_grad_copy(j).wait())
 
-    loop(0, n_dp, norm_wait)
-    total = jnp.maximum(jnp.sum(norms[...], axis=0), 0.0)
+    @pl.when(sec > 0)
+    def _():
+        total_copy(0).wait_recv()
+
+    total = jnp.maximum(total_in[...], 0.0)
     fac_out[...] = jnp.minimum(1.0, limit / jnp.sqrt(total + 1e-06))
 
     @pl.when(sec == 0)
     def _():
-        for q in range(n_sec):
-            def sent(d, q=q):
-                @pl.when((me != d) | (q != 0))
-                def _():
-                    norm_copy(q, d).wait_send()
-            loop(0, n_dp, sent)
+        loop(1, n_dp, lambda k: norm_copy(lax.rem(me + k, n_dp)).wait_send())
+        for q in range(1, n_sec):
+            total_copy(q).wait_send()
 
 
 def per_device(n_sec, n_dp, frozen, adapt_down, adapt_up, saved_inputs, out_grad, sensor, counts):
@@ -429,6 +465,7 @@
             pltpu.VMEM((1, 128), f32),
             pltpu.VMEM((1, 128), f32),
             pltpu.VMEM((n_dp, 1, 128), f32),
+            pltpu.VMEM((1, 128), f32),
             dma((n_dp,)),
             dma((2,)),
             dma((2, n_dp)),
@@ -443,8 +480,10 @@
             dma((n_dp,)),
             dma,
             dma,
-            dma((n_sec, n_dp)),
-            dma((n_dp,)),
+            dma((n_dp,)),
+            dma((n_dp,)),
+            dma((n_sec,)),
+            dma,
         ],
         compiler_params=pltpu.CompilerParams(
             collective_id=0, has_side_effects=True, vmem_limit_bytes=60 * 1024 * 1024

time: 77.6 us -> 78.4 us (1.010)
  Pallas kernels: 70.2 us -> 71 us
where the time goes in v3:
time: 78.4 us; the launch traced here: 78.2 us
  Pallas kernels  71 us (91%)
  other arithmetic  5.9 us (8%)
    pallas_call x1, Pallas kernels, per_device(): pl.pallas_call(functools.partial(chain_kernel, n_sec, n_dp, rank, pack, f...  71 us
    convert_element_type x1, other arithmetic, per_device(): up = (up.reshape(sen_local, rank, width) * scale).astype(bf)  3.51 us
    broadcast_in_dim x1, other arithmetic, per_device(): return (result[None, None], jnp.swapaxes(down, 1, 2)[None], up[None])  1.77 us

profile of v3, /device:TPU:0, one launch (start us, length us, event | category | flops | bytes accessed | tf_op | source)
XLA Modules:
  0.0 78.2 jit_solution(9969729080337687744)
XLA Ops:
  0.6 0.0 copy-start.2
  0.6 71.0 %chain.1 = (bf16[24,1024]{1,0:T(8,128)(2,1)}, bf16[128,8192]{1,0:T(8,128)(2,1)}, bf16[128,8192]{1,0:T(8,128)(2,1)}, f32[1,128]{1,0:T(1,128)}) custom-call(s32[1,8]{1,0:T(1,128)} %sensor.1, s32[2]{0:T(128)} %counts.1, bf16[1024,8192]{1,0:T(8,128)(2,1)} %bitcast.20, bf16[128,8192]{1,0:T(8,128)(2,1)} %bitcast.23, bf16[128,8192]{1,0:T(8,128)(2,1)} %bitcast.24, ...), custom_call_target="tpu_custom_call" | custom-call | tf_op jit(solution)/shard_map/chain/pallas_call | solution.py:438
  71.6 0.0 copy-done.2
  71.7 0.6 divide_multiply_fusion
  72.3 0.0 copy-start
  72.3 3.5 %fusion = bf16[1,2,64,8192]{3,2,1,0:T(8,128)(2,1)} fusion(bf16[1,2,64,8192]{3,2,1,0:T(8,128)(2,1)} %bitcast.22, f32[2]{0:T(128)S(1)} %divide_multiply_fusion), kind=kLoop, calls=%fused_computation.1 | loop fusion | flops 3145728 | bytes 4194312 | tf_op jit(solution)/shard_map/convert_element_type | solution.py:503
  75.8 0.0 copy-done
  75.8 0.0 copy-start.1
  75.8 1.8 %fusion.2 = bf16[1,2,8192,64]{2,3,1,0:T(8,128)(2,1)} fusion(bf16[2,64,8192]{2,1,0:T(8,128)(2,1)S(1)} %bitcast.21, f32[2]{0:T(128)S(1)} %divide_multiply_fusion), kind=kLoop, calls=%fused_computation.4 | loop fusion | flops 3145728 | bytes 4194312 | tf_op jit(solution)/shard_map/broadcast_in_dim | solution.py:504
  77.6 0.0 copy-done.1
  77.6 0.6 copy.11
Async XLA Ops:
  0.6 71.0 %copy-start.2 = (s32[2]{0:T(128)S(1)}, s32[2]{0:T(128)}, u32[]{:S(2)}) copy-start(s32[2]{0:T(128)} %counts.1) | copy-start | bytes 28
  72.3 3.5 %copy-start = (bf16[128,8192]{1,0:T(8,128)(2,1)S(1)}, bf16[128,8192]{1,0:T(8,128)(2,1)}, u32[]{:S(2)}) copy-start(bf16[128,8192]{1,0:T(8,128)(2,1)} %get-tuple-element.8) | copy-start | bytes 6291460
  75.8 1.8 %copy-start.1 = (bf16[24,1024]{1,0:T(8,128)(2,1)S(1)}, bf16[24,1024]{1,0:T(8,128)(2,1)}, u32[]{:S(2)}) copy-start(bf16[24,1024]{1,0:T(8,128)(2,1)} %get-tuple-element.7) | copy-start | bytes 147460
